TPU v7x, 512 devices: a whole 4x4x16 slice. The times are simulated.
512 devices in a mesh: row: 16 (over x_hi, y, core), col: 32 (over z, x_lo).
Axes of the slice: x: 4 (x_hi: 2, x_lo: 2; x = x_hi * 2 + x_lo), y: 4, z: 16, core: 2. Of those that a mesh axis runs over, the one named last changes fastest.
Arguments:
- left_panel: bfloat16 [256, 512, 32], P('col', 'row'), may hold values from -6 to 6
- right_panel: bfloat16 [256, 512, 32], P('row', 'col'), may hold values from -6 to 6
- pair_grad: bfloat16 [512, 512, 128], P('row', 'col'), may hold values from -24 to 24
- out_weight: bfloat16 [1024, 128], replicated, may hold values from -0.1875 to 0.1875
Outputs:
- left_grad: float32 [256, 512, 32], P('col', 'row')
- right_grad: float32 [256, 512, 32], P('row', 'col')
- weight_grad: float32 [1024, 128], replicated
All inputs are finite; a program needn't handle non-finite values.
Results may differ from a plain program's by a relative error of at most 0.0033.
Values may be sent and summed in bfloat16 or wider, within the bound.
A program may use at most 64 MiB of HBM per device.

v0:
```python
import jax
import jax.numpy as jnp
from jax import lax
from jax.sharding import PartitionSpec as P

N = 512


def from_everyone(array, axis):
    peers = lax.axis_size(axis)
    return lax.all_to_all(
        jnp.broadcast_to(array[None], (peers, *array.shape)), axis, 0, 0, tiled=True
    )


def joined_along(blocks, dim):
    shape = list(blocks.shape[1:])
    shape[dim] *= blocks.shape[0]
    return jnp.moveaxis(blocks, 0, dim).reshape(shape)


def collect(array, axis, dim):
    blocks = from_everyone(array, axis)
    return joined_along(blocks, dim)


def split_up(array, dim, peers):
    before, after = (array.shape[:dim], array.shape[dim + 1 :])
    return jnp.moveaxis(array.reshape(*before, peers, -1, *after), dim, 0)


def summed_on_arrival(array, axis, dim):
    peers = lax.axis_size(axis)
    blocks = lax.all_to_all(split_up(array, dim, peers), axis, 0, 0, tiled=True)
    return jnp.sum(blocks, axis=0)


def padded_to(lines, peers):
    spare = -lines.shape[0] % peers
    if not spare:
        return lines
    return jnp.concatenate([lines, jnp.zeros((spare, *lines.shape[1:]), lines.dtype)])


def total_of(array, axes):
    lines = array.reshape(-1, array.shape[-1])
    own = summed_on_arrival(padded_to(lines, lax.axis_size(axes)), axes, 0)
    whole = collect(own, axes, 0)
    return whole[: len(lines)].reshape(array.shape)


def per_device(left_panel, right_panel, pair_grad, out_weight):
    whole_left = collect(left_panel, "col", 0)
    whole_right = collect(right_panel, "row", 0)
    sequences, rows_here, channels = whole_left.shape
    cols_here = whole_right.shape[1]
    pair_width = pair_grad.shape[2]
    block_rows = 16
    blocks_total = rows_here // block_rows
    right_flat = whole_right.reshape(sequences, cols_here * channels)
    weight_t = out_weight.T

    def advance(carried, block_index):
        right_acc, weight_acc = carried
        first_row = block_index * block_rows
        grad_rows = lax.dynamic_slice_in_dim(pair_grad, first_row, block_rows, 0).reshape(
            block_rows * cols_here, pair_width
        )
        left_rows = lax.dynamic_slice_in_dim(whole_left, first_row, block_rows, 1).reshape(
            sequences, block_rows * channels
        )
        expanded = (
            jnp.dot(grad_rows, weight_t, preferred_element_type=jnp.float32) / sequences
        ).astype(jnp.bfloat16)
        expanded = (
            expanded.reshape(block_rows, cols_here, channels, channels)
            .transpose(0, 2, 1, 3)
            .reshape(block_rows * channels, cols_here * channels)
        )
        left_term = lax.dot_general(
            right_flat, expanded, (((1,), (1,)), ((), ())), preferred_element_type=jnp.float32
        )
        right_acc = right_acc + jnp.dot(left_rows, expanded, preferred_element_type=jnp.float32)
        outer_prod = lax.dot_general(
            left_rows, right_flat, (((0,), (0,)), ((), ())), preferred_element_type=jnp.float32
        )
        outer_prod = (outer_prod / sequences).astype(jnp.bfloat16)
        outer_prod = (
            outer_prod.reshape(block_rows, channels, cols_here, channels)
            .transpose(0, 2, 1, 3)
            .reshape(block_rows * cols_here, channels * channels)
        )
        weight_acc = weight_acc + lax.dot_general(
            outer_prod, grad_rows, (((0,), (0,)), ((), ())), preferred_element_type=jnp.float32
        )
        left_term = summed_on_arrival(left_term, "col", 0)
        return ((right_acc, weight_acc), left_term)

    start_state = (
        jnp.zeros((sequences, cols_here * channels), jnp.float32),
        jnp.zeros(out_weight.shape, jnp.float32),
    )
    (right_acc, weight_acc), left_terms = lax.scan(
        advance, start_state, jnp.arange(blocks_total, dtype=jnp.int32)
    )
    left_grad = (
        left_terms.reshape(blocks_total, -1, block_rows, channels)
        .transpose(1, 0, 2, 3)
        .reshape(-1, rows_here, channels)
    )
    right_grad = summed_on_arrival(right_acc, "row", 0).reshape(-1, cols_here, channels)
    weight_total = total_of(total_of(weight_acc, "col"), "row")
    return (left_grad, right_grad, weight_total / N)


def solution(mesh):
    in_specs = (P("col", "row", None), P("row", "col", None), P("row", "col", None), P())
    out_specs = (P("col", "row", None), P("row", "col", None), P())
    return jax.shard_map(
        per_device, mesh=mesh, in_specs=in_specs, out_specs=out_specs, check_vma=False
    )
```

profile of v0, /device:TPU:1, one launch (start us, length us, event | category | flops | bytes accessed | tf_op | source)
XLA Modules:
  0.0 289.5 jit_solution(3001188788535580214)
XLA Ops:
  0.6 0.0 copy-start.7
  0.6 1.1 broadcast_in_dim.41
  1.7 1.7 reshape.69
  3.4 10.2 %all-to-all-start.2 = ((bf16[16,2,4096]{2,1,0:T(2,128)(2,1)}), bf16[16,2,4096]{2,1,0:T(2,128)(2,1)S(1)}, u32[]{:S(2)}, u32[]{:S(2)}) async-start(bf16[16,2,4096]{2,1,0:T(2,128)(2,1)} %reshape.69), calls=%async_computation.2 | async-start | bytes 524288 | tf_op jit(solution)/shard_map/all_to_all | solution.py:11
  13.6 0.5 broadcast_in_dim.40
  14.1 0.0 copy-start.6
  14.1 2.7 reshape.67
  16.8 5.6 %all-to-all-done.2 = bf16[16,2,4096]{2,1,0:T(2,128)(2,1)S(1)} async-done(((bf16[16,2,4096]{2,1,0:T(2,128)(2,1)}), bf16[16,2,4096]{2,1,0:T(2,128)(2,1)S(1)}, u32[]{:S(2)}, u32[]{:S(2)}) %all-to-all-start.2) | async-done | bytes 262176 | tf_op jit(solution)/shard_map/all_to_all | solution.py:11
  22.3 13.6 %all-to-all-start.1 = ((bf16[32,2,4096]{2,1,0:T(2,128)(2,1)}), bf16[32,2,4096]{2,1,0:T(2,128)(2,1)S(1)}, u32[]{:S(2)}, u32[]{:S(2)}) async-start(bf16[32,2,4096]{2,1,0:T(2,128)(2,1)} %reshape.67), calls=%async_computation.1 | async-start | bytes 1048576 | tf_op jit(solution)/shard_map/all_to_all | solution.py:11
  36.0 0.0 copy-done.6
  36.0 0.1 copy.21
  36.1 0.5 reshape.70
  36.6 1.7 reshape_reshape.6
  38.4 28.2 %all-to-all-done.1 = bf16[32,2,4096]{2,1,0:T(2,128)(2,1)S(1)} async-done(((bf16[32,2,4096]{2,1,0:T(2,128)(2,1)}), bf16[32,2,4096]{2,1,0:T(2,128)(2,1)S(1)}, u32[]{:S(2)}, u32[]{:S(2)}) %all-to-all-start.1) | async-done | bytes 524320 | tf_op jit(solution)/shard_map/all_to_all | solution.py:11
  66.5 1.0 reshape.68
  67.5 1.7 copy.22
  69.2 94.8 %while.15 = (s32[]{:T(128)}, f32[256,512]{1,0:T(8,128)}, f32[1024,128]{1,0:T(8,128)}, f32[2,8,512]{2,1,0:T(8,128)S(1)}, s32[2]{0:T(128)S(1)}, /*index=5*/bf16[25...) while((s32[]{:T(128)}, f32[256,512]{1,0:T(8,128)}, ...), condition=%wide.region_2.3_spmd.clone, body=%wide.region_0.2_spmd.clone.sunk | while | flops 538570752 | bytes 26263976 | solution.py:103
  69.3 0.7 dynamic_slice.20
  70.6 0.8 constant_dynamic-slice_fusion.5
  71.5 0.3 fusion.34
  71.8 1.6 reshape.75
  73.3 2.2 copy.30
  75.6 3.4 %reshape.76 = bf16[512,512]{1,0:T(8,128)(2,1)S(1)} reshape(bf16[16,32,16,32]{3,2,1,0:T(8,128)(2,1)} %bitcast.74) | data formatting | bytes 1048576 | tf_op jit(solution)/shard_map/while/body/eval_jaxpr/reshape | solution.py:78
  78.9 2.1 convolution_bitcast_fusion.2
  81.0 5.2 %all-to-all-start = ((f32[32,8,512]{2,1,0:T(8,128)}), f32[32,8,512]{2,1,0:T(8,128)}, u32[]{:S(2)}, u32[]{:S(2)}) async-start(f32[32,8,512]{2,1,0:T(8,128)} %convolution_bitcast_fusion.2), calls=%async_computation | async-start | bytes 1048576 | tf_op jit(solution)/shard_map/while/body/eval_jaxpr/all_to_all | solution.py:34
  86.3 1.2 fusion.35
  87.5 1.2 reshape.77
  88.7 1.9 copy.31
  90.6 3.6 %reshape.78 = bf16[256,1024]{1,0:T(8,128)(2,1)S(1)} reshape(bf16[16,16,32,32]{3,2,1,0:T(8,128)(2,1)} %bitcast.75) | data formatting | bytes 1048576 | tf_op jit(solution)/shard_map/while/body/eval_jaxpr/reshape | solution.py:91
  94.3 0.5 convolution_add_fusion.5
  94.7 1.1 convolution_add_fusion.4
  95.9 19.7 %all-to-all-done = f32[32,8,512]{2,1,0:T(8,128)} async-done(((f32[32,8,512]{2,1,0:T(8,128)}), f32[32,8,512]{2,1,0:T(8,128)}, u32[]{:S(2)}, u32[]{:S(2)}) %all-to-all-start) | async-done | bytes 524320 | tf_op jit(solution)/shard_map/while/body/eval_jaxpr/all_to_all | solution.py:34
  115.6 1.1 reduce_sum.41
  116.7 0.0 copy-start.2
  116.7 0.0 copy-start.4
  116.7 0.7 dynamic_slice.20
  118.1 0.8 constant_dynamic-slice_fusion.5
  118.9 0.3 fusion.34
  119.2 1.6 reshape.75
  120.8 2.2 copy.30
  123.0 3.4 %reshape.76 = bf16[512,512]{1,0:T(8,128)(2,1)S(1)} reshape(bf16[16,32,16,32]{3,2,1,0:T(8,128)(2,1)} %bitcast.74) | data formatting | bytes 1048576 | tf_op jit(solution)/shard_map/while/body/eval_jaxpr/reshape | solution.py:78
  126.4 2.1 convolution_bitcast_fusion.2
  128.5 5.9 %all-to-all-start = ((f32[32,8,512]{2,1,0:T(8,128)}), f32[32,8,512]{2,1,0:T(8,128)}, u32[]{:S(2)}, u32[]{:S(2)}) async-start(f32[32,8,512]{2,1,0:T(8,128)} %convolution_bitcast_fusion.2), calls=%async_computation | async-start | bytes 1048576 | tf_op jit(solution)/shard_map/while/body/eval_jaxpr/all_to_all | solution.py:34
  134.4 1.2 fusion.35
  135.7 1.2 reshape.77
  136.9 1.9 copy.31
  138.8 3.6 %reshape.78 = bf16[256,1024]{1,0:T(8,128)(2,1)S(1)} reshape(bf16[16,16,32,32]{3,2,1,0:T(8,128)(2,1)} %bitcast.75) | data formatting | bytes 1048576 | tf_op jit(solution)/shard_map/while/body/eval_jaxpr/reshape | solution.py:91
  142.4 0.5 convolution_add_fusion.5
  142.9 2.4 convolution_add_fusion.4
  145.3 17.7 %all-to-all-done = f32[32,8,512]{2,1,0:T(8,128)} async-done(((f32[32,8,512]{2,1,0:T(8,128)}), f32[32,8,512]{2,1,0:T(8,128)}, u32[]{:S(2)}, u32[]{:S(2)}) %all-to-all-start) | async-done | bytes 524320 | tf_op jit(solution)/shard_map/while/body/eval_jaxpr/all_to_all | solution.py:34
  162.9 1.1 reduce_sum.41
  164.1 35.7 %all_to_all.42 = f32[32,32,128]{2,1,0:T(8,128)S(1)} all-to-all(f32[32,32,128]{2,1,0:T(8,128)} %bitcast.78), channel_id=1, replica_groups=mesh['row'=16,'col'=32] {'col'}, dimensions={0} | all-to-all | bytes 1048576 | tf_op jit(solution)/shard_map/all_to_all | solution.py:34
  199.8 0.1 broadcast_in_dim.42
  199.8 36.2 %all_to_all.43 = f32[32,32,128]{2,1,0:T(8,128)S(1)} all-to-all(f32[32,32,128]{2,1,0:T(8,128)S(1)} %broadcast_in_dim.42), channel_id=1, replica_groups=mesh['row'=16,'col'=32] {'col'}, dimensions={0} | all-to-all | bytes 1048576 | tf_op jit(solution)/shard_map/all_to_all | solution.py:11
  236.0 19.9 %all_to_all.44 = f32[16,64,128]{2,1,0:T(8,128)S(1)} all-to-all(f32[16,64,128]{2,1,0:T(8,128)S(1)} %bitcast.83), channel_id=1, replica_groups=mesh['row'=16,'col'=32] {'row'}, dimensions={0} | all-to-all | bytes 1048576 | tf_op jit(solution)/shard_map/all_to_all | solution.py:34
  256.0 4.5 %all-to-all-start.3 = ((f32[16,16,512]{2,1,0:T(8,128)}), f32[16,16,512]{2,1,0:T(8,128)S(1)}, u32[]{:S(2)}, u32[]{:S(2)}) async-start(f32[16,16,512]{2,1,0:T(8,128)} %bitcast.4), calls=%async_computation.3 | async-start | bytes 1048576 | tf_op jit(solution)/shard_map/all_to_all | solution.py:34
  260.5 11.3 %all-to-all-done.3 = f32[16,16,512]{2,1,0:T(8,128)S(1)} async-done(((f32[16,16,512]{2,1,0:T(8,128)}), f32[16,16,512]{2,1,0:T(8,128)S(1)}, u32[]{:S(2)}, u32[]{:S(2)}) %all-to-all-start.3) | async-done | bytes 524320 | tf_op jit(solution)/shard_map/all_to_all | solution.py:34
  271.9 0.8 broadcast_in_dim.43
  272.7 4.5 %all-to-all-start.7 = ((f32[16,64,128]{2,1,0:T(8,128)}), f32[16,64,128]{2,1,0:T(8,128)S(1)}, u32[]{:S(2)}, u32[]{:S(2)}) async-start(f32[16,64,128]{2,1,0:T(8,128)} %broadcast_in_dim.43), calls=%async_computation.7 | async-start | bytes 1048576 | tf_op jit(solution)/shard_map/all_to_all | solution.py:11
  277.2 0.1 reshape.55
  277.3 0.7 copy.23
  278.0 0.7 reshape.58
  278.8 9.8 %all-to-all-done.7 = f32[16,64,128]{2,1,0:T(8,128)S(1)} async-done(((f32[16,64,128]{2,1,0:T(8,128)}), f32[16,64,128]{2,1,0:T(8,128)S(1)}, u32[]{:S(2)}, u32[]{:S(2)}) %all-to-all-start.7) | async-done | bytes 524320 | tf_op jit(solution)/shard_map/all_to_all | solution.py:11
  288.6 0.8 broadcast_multiply_fusion
  (34 shorter events, 0.2 us)
Async XLA Ops:
  0.6 13.0 %copy-start.7 = (bf16[8,32,32]{2,1,0:T(8,128)(2,1)S(1)}, bf16[8,32,32]{2,1,0:T(8,128)(2,1)}, u32[]{:S(2)}) copy-start(bf16[8,32,32]{2,1,0:T(8,128)(2,1)} %param.6) | copy-start | bytes 49156
  3.4 18.9 %all-to-all-start.2 = ((bf16[16,2,4096]{2,1,0:T(2,128)(2,1)}), bf16[16,2,4096]{2,1,0:T(2,128)(2,1)S(1)}, u32[]{:S(2)}, u32[]{:S(2)}) async-start(bf16[16,2,4096]{2,1,0:T(2,128)(2,1)} %reshape.69), calls=%async_computation.2 | async-start | bytes 524288 | tf_op jit(solution)/shard_map/all_to_all | solution.py:11
  14.1 21.9 %copy-start.6 = (bf16[1024,128]{1,0:T(8,128)(2,1)S(1)}, bf16[1024,128]{1,0:T(8,128)(2,1)}, u32[]{:S(2)}) copy-start(bf16[1024,128]{1,0:T(8,128)(2,1)} %param.9) | copy-start | bytes 786436
  22.3 44.2 %all-to-all-start.1 = ((bf16[32,2,4096]{2,1,0:T(2,128)(2,1)}), bf16[32,2,4096]{2,1,0:T(2,128)(2,1)S(1)}, u32[]{:S(2)}, u32[]{:S(2)}) async-start(bf16[32,2,4096]{2,1,0:T(2,128)(2,1)} %reshape.67), calls=%async_computation.1 | async-start | bytes 1048576 | tf_op jit(solution)/shard_map/all_to_all | solution.py:11
  69.3 6.3 %copy-start.2 = (bf16[128,1024]{1,0:T(8,128)(2,1)}, bf16[128,1024]{1,0:T(8,128)(2,1)S(1)}, u32[]{:S(2)}) copy-start(bf16[128,1024]{1,0:T(8,128)(2,1)S(1)} %get-tuple-element.211) | copy-start | bytes 786436 | tf_op jit(solution)/shard_map/while
  69.3 17.0 %copy-start.4 = (bf16[256,32,32]{0,2,1:T(8,128)(2,1)}, bf16[256,32,32]{0,2,1:T(8,128)(2,1)S(1)}, u32[]{:S(2)}) copy-start(bf16[256,32,32]{0,2,1:T(8,128)(2,1)S(1)} %get-tuple-element.209) | copy-start | bytes 1572868 | tf_op jit(solution)/shard_map/while
  81.0 34.6 %all-to-all-start = ((f32[32,8,512]{2,1,0:T(8,128)}), f32[32,8,512]{2,1,0:T(8,128)}, u32[]{:S(2)}, u32[]{:S(2)}) async-start(f32[32,8,512]{2,1,0:T(8,128)} %convolution_bitcast_fusion.2), calls=%async_computation | async-start | bytes 1048576 | tf_op jit(solution)/shard_map/while/body/eval_jaxpr/all_to_all | solution.py:34
  90.6 3.6 %copy-start = (f32[1024,128]{1,0:T(8,128)S(1)}, f32[1024,128]{1,0:T(8,128)}, u32[]{:S(2)}) copy-start(f32[1024,128]{1,0:T(8,128)} %get-tuple-element.192) | copy-start | bytes 1572868 | tf_op jit(solution)/shard_map/while
  94.2 22.5 %copy-start.3 = (bf16[128,1024]{1,0:T(8,128)(2,1)S(1)}, bf16[128,1024]{1,0:T(8,128)(2,1)}, u32[]{:S(2)}) copy-start(bf16[128,1024]{1,0:T(8,128)(2,1)} %copy-done.2) | copy-start | bytes 786436 | tf_op jit(solution)/shard_map/while
  94.2 22.5 %copy-start.5 = (bf16[256,32,32]{0,2,1:T(8,128)(2,1)S(1)}, bf16[256,32,32]{0,2,1:T(8,128)(2,1)}, u32[]{:S(2)}) copy-start(bf16[256,32,32]{0,2,1:T(8,128)(2,1)} %copy-done.4) | copy-start | bytes 1572868 | tf_op jit(solution)/shard_map/while
  94.7 22.0 %copy-start.1 = (f32[1024,128]{1,0:T(8,128)}, f32[1024,128]{1,0:T(8,128)S(1)}, u32[]{:S(2)}) copy-start(f32[1024,128]{1,0:T(8,128)S(1)} %convolution_add_fusion.5) | copy-start | bytes 1572868 | tf_op jit(solution)/shard_map/while
  116.7 6.3 %copy-start.2 = (bf16[128,1024]{1,0:T(8,128)(2,1)}, bf16[128,1024]{1,0:T(8,128)(2,1)S(1)}, u32[]{:S(2)}) copy-start(bf16[128,1024]{1,0:T(8,128)(2,1)S(1)} %get-tuple-element.211) | copy-start | bytes 786436 | tf_op jit(solution)/shard_map/while
  116.7 17.7 %copy-start.4 = (bf16[256,32,32]{0,2,1:T(8,128)(2,1)}, bf16[256,32,32]{0,2,1:T(8,128)(2,1)S(1)}, u32[]{:S(2)}) copy-start(bf16[256,32,32]{0,2,1:T(8,128)(2,1)S(1)} %get-tuple-element.209) | copy-start | bytes 1572868 | tf_op jit(solution)/shard_map/while
  128.5 34.5 %all-to-all-start = ((f32[32,8,512]{2,1,0:T(8,128)}), f32[32,8,512]{2,1,0:T(8,128)}, u32[]{:S(2)}, u32[]{:S(2)}) async-start(f32[32,8,512]{2,1,0:T(8,128)} %convolution_bitcast_fusion.2), calls=%async_computation | async-start | bytes 1048576 | tf_op jit(solution)/shard_map/while/body/eval_jaxpr/all_to_all | solution.py:34
  138.8 3.6 %copy-start = (f32[1024,128]{1,0:T(8,128)S(1)}, f32[1024,128]{1,0:T(8,128)}, u32[]{:S(2)}) copy-start(f32[1024,128]{1,0:T(8,128)} %get-tuple-element.192) | copy-start | bytes 1572868 | tf_op jit(solution)/shard_map/while
  142.4 21.6 %copy-start.3 = (bf16[128,1024]{1,0:T(8,128)(2,1)S(1)}, bf16[128,1024]{1,0:T(8,128)(2,1)}, u32[]{:S(2)}) copy-start(bf16[128,1024]{1,0:T(8,128)(2,1)} %copy-done.2) | copy-start | bytes 786436 | tf_op jit(solution)/shard_map/while
  142.4 21.6 %copy-start.5 = (bf16[256,32,32]{0,2,1:T(8,128)(2,1)S(1)}, bf16[256,32,32]{0,2,1:T(8,128)(2,1)}, u32[]{:S(2)}) copy-start(bf16[256,32,32]{0,2,1:T(8,128)(2,1)} %copy-done.4) | copy-start | bytes 1572868 | tf_op jit(solution)/shard_map/while
  142.9 21.1 %copy-start.1 = (f32[1024,128]{1,0:T(8,128)}, f32[1024,128]{1,0:T(8,128)S(1)}, u32[]{:S(2)}) copy-start(f32[1024,128]{1,0:T(8,128)S(1)} %convolution_add_fusion.5) | copy-start | bytes 1572868 | tf_op jit(solution)/shard_map/while
  256.0 15.9 %all-to-all-start.3 = ((f32[16,16,512]{2,1,0:T(8,128)}), f32[16,16,512]{2,1,0:T(8,128)S(1)}, u32[]{:S(2)}, u32[]{:S(2)}) async-start(f32[16,16,512]{2,1,0:T(8,128)} %bitcast.4), calls=%async_computation.3 | async-start | bytes 1048576 | tf_op jit(solution)/shard_map/all_to_all | solution.py:34
  272.7 15.9 %all-to-all-start.7 = ((f32[16,64,128]{2,1,0:T(8,128)}), f32[16,64,128]{2,1,0:T(8,128)S(1)}, u32[]{:S(2)}, u32[]{:S(2)}) async-start(f32[16,64,128]{2,1,0:T(8,128)} %broadcast_in_dim.43), calls=%async_computation.7 | async-start | bytes 1048576 | tf_op jit(solution)/shard_map/all_to_all | solution.py:11
where the time goes:
time: 291 us; the launch traced here: 289 us
  waiting for transfers between devices  92.3 us (32%)
  blocking collectives  91.8 us (32%)
  local copies, waits for them, and re-layouts  44.3 us (15%)
  starting transfers between devices  44 us (15%)
  matrix products  11.6 us (4%)
  other arithmetic  3.13 us (1%)
    all_to_all x2, blocking collectives, summed_on_arrival(): blocks = lax.all_to_all(split_up(array, dim, peers), axis, 0, 0, tiled=True)  55.6 us
    all_to_all x3, waiting for transfers between devices, summed_on_arrival(): blocks = lax.all_to_all(split_up(array, dim, peers), axis, 0, 0, tiled=True)  48.7 us
    all_to_all x3, waiting for transfers between devices, from_everyone(): lax.all_to_all(jnp.broadcast_to(array[None], (peers, *array.shape)), axis...  43.5 us
    all_to_all x1, blocking collectives, from_everyone(): lax.all_to_all(jnp.broadcast_to(array[None], (peers, *array.shape)), axis...  36.2 us
    all_to_all x3, starting transfers between devices, from_everyone(): lax.all_to_all(jnp.broadcast_to(array[None], (peers, *array.shape)), axis...  28.3 us
    all_to_all x3, starting transfers between devices, summed_on_arrival(): blocks = lax.all_to_all(split_up(array, dim, peers), axis, 0, 0, tiled=True)  15.7 us
    unnamed x10, local copies, waits for them, and re-layouts  7.75 us
    reshape x4, local copies, waits for them, and re-layouts, advance(): expanded.reshape(block_rows, cols_here, channels, channels)  7.6 us
  transfers between devices with their start and end apart: 6, of which 6 were waited for; matrix products, arithmetic and copies ran while one was open for 9% of the time, Pallas kernels for 0%

commit v1 on v0

v1 whole, which is shorter than its diff:
```python
import functools

import jax
import jax.numpy as jnp
from jax import lax
from jax.experimental import pallas as pl
from jax.experimental.pallas import tpu as pltpu
from jax.sharding import PartitionSpec as P

MESH = pl.DeviceIdType.MESH
F32, BF = jnp.float32, jnp.bfloat16
ROWS, ZS, XL = 16, 16, 2
COLS = ZS * XL
PLANE = ROWS * XL


def swap4(x):
    lane = lax.broadcasted_iota(jnp.int32, x[0].shape, 1)
    low = lane < 64
    even = (lane // 32) % 2 == 0
    r = [pltpu.roll(v, 64, 1) for v in x]
    a = [
        jnp.where(low, x[0], r[2]),
        jnp.where(low, x[1], r[3]),
        jnp.where(low, r[0], x[2]),
        jnp.where(low, r[1], x[3]),
    ]
    y = []
    for p in (0, 2):
        y.append(jnp.where(even, a[p], pltpu.roll(a[p + 1], 32, 1)))
        y.append(jnp.where(even, pltpu.roll(a[p], 96, 1), a[p + 1]))
    return y


def expand(g, w, tile, ef, eb):
    def part(a, _):
        rows = pl.ds(pl.multiple_of(a * 128, 128), 128)
        tile[...] = lax.dot_general(
            g[...], w[rows, :], (((1,), (1,)), ((), ())), preferred_element_type=F32
        ) * (1.0 / 256)
        for jg in range(4):
            for i0 in range(4):
                x = [tile[pl.ds(i0 * 128 + 4 * jg + b, 8, stride=16), :] for b in range(4)]
                y = swap4(x)
                for q in range(4):
                    ef[jg, pl.ds(i0 * 256 + 4 * a + q, 8, stride=32), :] = y[q]
        return 0

    lax.fori_loop(0, 8, part, 0)

    def cast(t, _):
        rows = pl.ds(pl.multiple_of(t * 128, 128), 128)
        for jg in range(4):
            eb[rows, jg * 128 : (jg + 1) * 128] = ef[jg, rows, :].astype(BF)
        return 0

    lax.fori_loop(0, 8, cast, 0)


def left_term(rg, eb, out):
    def part(t, _):
        rows = pl.ds(pl.multiple_of(t * 256, 256), 256)
        v = lax.dot_general(rg[...], eb[rows, :], (((1,), (1,)), ((), ())), preferred_element_type=F32)
        out[:, :, rows] = v.reshape(32, 8, 256).astype(BF)
        return 0

    lax.fori_loop(0, 4, part, 0)


def right_term(lg, eb, out):
    def part(t, _):
        cols = pl.ds(pl.multiple_of(t * 256, 256), 256)
        v = jnp.dot(lg[...], eb[:, cols], preferred_element_type=F32)
        out[:, :, cols] = v.reshape(16, 16, 256).astype(BF)
        return 0

    lax.fori_loop(0, 2, part, 0)


def outer_part(lg, rg, of):
    def part(t, _):
        cols = pl.ds(pl.multiple_of(t * 256, 256), 256)
        for h in range(2):
            v = lax.dot_general(
                lg[:, cols],
                rg[:, h * 256 : (h + 1) * 256],
                (((0,), (0,)), ((), ())),
                preferred_element_type=F32,
            ) * (1.0 / 256)
            of[2 * h, cols, :] = v[:, :128]
            of[2 * h + 1, cols, :] = v[:, 128:]
        return 0

    lax.fori_loop(0, 4, part, 0)


def weight_part(g, of, tile, out):
    def part(a, _):
        for jg in range(4):
            for i0 in range(4):
                x = [of[jg, pl.ds(i0 * 256 + 4 * a + q, 8, stride=32), :] for q in range(4)]
                y = swap4(x)
                for b in range(4):
                    tile[pl.ds(i0 * 128 + 4 * jg + b, 8, stride=16), :] = y[b]
        v = lax.dot_general(
            tile[...].astype(BF), g[...], (((0,), (0,)), ((), ())), preferred_element_type=F32
        )
        out[pl.ds(a * 4, 4)] = v.reshape(4, 32, 128).astype(BF)
        return 0

    lax.fori_loop(0, 8, part, 0)


def kernel(
    l_hbm, r_hbm, g_hbm, w_hbm, lo, ro, wo,
    lv, rv, gv, wv, lf, rf, lflat, rflat, g2,
    lb, rb, lg, rg, tile, ef, eb, of,
    sl, rl, sr, rr, sw, rw, zb, ab,
    in_sem, ag_l, ag_r, rs_l, rs_r, rs_w, z_w, ag_w,
):
    row, col = lax.axis_index("row"), lax.axis_index("col")
    z, xl = col // XL, col % XL
    plane = xl * ROWS + row

    def col_at(k):
        c = ((z + k // XL) % ZS) * XL + (xl + k % XL) % XL
        return {"row": row, "col": c}, c

    def row_at(k):
        r = (row + k) % ROWS
        return {"row": r, "col": col}, r

    def plane_at(k):
        r, x = (row + k % ROWS) % ROWS, (xl + k // ROWS) % XL
        return {"row": r, "col": z * XL + x}, x * ROWS + r

    def z_at(k):
        zz = (z + k) % ZS
        return {"row": row, "col": zz * XL + xl}, zz

    inputs = [
        pltpu.make_async_copy(src, dst, in_sem.at[n])
        for n, (src, dst) in enumerate(((l_hbm, lv), (r_hbm, rv), (g_hbm, gv), (w_hbm, wv)))
    ]
    for c in inputs:
        c.start()

    barrier = pltpu.get_barrier_semaphore()

    def greet(at, first, last):
        def one(k, _):
            pl.semaphore_signal(barrier, inc=1, device_id=at(k)[0], device_id_type=MESH)
            return 0

        lax.fori_loop(first, last, one, 0)

    greet(col_at, 1, COLS)
    greet(row_at, 1, ROWS)
    greet(plane_at, ROWS + 1, PLANE)

    inputs[0].wait()
    inputs[1].wait()
    lf[...] = lv[...].reshape(256, 32).astype(F32)
    rf[...] = rv[...].reshape(256, 32).astype(F32)
    for i in range(32):
        lflat[:, 32 * i : 32 * i + 32] = lf[pl.ds(i, 8, stride=32), :]
    for j in range(16):
        rflat[:, 32 * j : 32 * j + 32] = rf[pl.ds(j, 16, stride=16), :]
    lb[col] = lflat[...].astype(BF)
    rb[row] = rflat[...].astype(BF)

    inputs[2].wait()
    inputs[3].wait()
    g2[...] = gv[...].reshape(512, 128)
    expand(g2, wv, tile, ef, eb)

    pl.semaphore_wait(barrier, COLS - 1 + ROWS - 1 + PLANE - ROWS - 1)

    def copies(at, n, src_slot, dst_slot, sems):
        def make(k):
            where, slot = at(k)
            return pltpu.make_async_remote_copy(
                src_ref=src_slot(slot),
                dst_ref=dst_slot,
                send_sem=sems.at[0, k],
                recv_sem=sems.at[1, k],
                device_id=where,
                device_id_type=MESH,
            )

        def each(act):
            def one(k, _):
                act(make(k))
                return 0

            lax.fori_loop(1, n, one, 0)

        return (
            lambda: each(lambda c: c.start()),
            lambda: each(lambda c: c.wait_recv()),
            lambda: each(lambda c: c.wait_send()),
        )

    ag_r_start, ag_r_recv, ag_r_sent = copies(row_at, ROWS, lambda s: rb.at[row], rb.at[row], ag_r)
    ag_l_start, ag_l_recv, ag_l_sent = copies(col_at, COLS, lambda s: lb.at[col], lb.at[col], ag_l)
    rs_l_start, rs_l_recv, rs_l_sent = copies(col_at, COLS, lambda s: sl.at[s], rl.at[col], rs_l)
    rs_r_start, rs_r_recv, rs_r_sent = copies(row_at, ROWS, lambda s: sr.at[s], rr.at[row], rs_r)
    rs_w_start, rs_w_recv, rs_w_sent = copies(plane_at, PLANE, lambda s: sw.at[s], rw.at[plane], rs_w)
    z_w_start, z_w_recv, z_w_sent = copies(z_at, ZS, lambda s: zb.at[z], zb.at[z], z_w)
    ag_w_start, ag_w_recv, ag_w_sent = copies(plane_at, PLANE, lambda s: ab.at[plane], ab.at[plane], ag_w)

    ag_r_start()
    ag_l_start()
    ag_r_recv()
    rg[...] = rb[...].reshape(256, 512)
    left_term(rg, eb, sl)
    rs_l_start()
    rl[col] = sl[col]
    ag_l_recv()
    lg[...] = lb[...].astype(F32).reshape(256, 1024).astype(BF)
    outer_part(lg, rg, of)
    weight_part(g2, of, tile, sw)
    rs_w_start()
    rw[plane] = sw[plane]
    right_term(lg, eb, sr)
    rs_r_start()
    rr[row] = sr[row]
    rs_w_recv()
    zb[z] = jnp.sum(rw[...].astype(F32), axis=0).astype(BF)
    z_w_start()
    rs_r_recv()
    rflat[...] = jnp.sum(rr[...].astype(F32), axis=0)
    for j in range(16):
        ro[:, j, :] = rflat[:, 32 * j : 32 * j + 32]
    z_w_recv()
    ab[plane] = jnp.sum(zb[...].astype(F32), axis=0).astype(BF)
    ag_w_start()
    rs_l_recv()
    lflat[...] = jnp.sum(rl[...].astype(F32), axis=0)
    for i in range(32):
        lo[:, i, :] = lflat[:, 32 * i : 32 * i + 32]
    ag_w_recv()
    wo[...] = ab[...].astype(F32).reshape(1024, 128) * (1.0 / 512)
    for done in (ag_r_sent, ag_l_sent, rs_l_sent, rs_r_sent, rs_w_sent, z_w_sent, ag_w_sent):
        done()


def per_device(left_panel, right_panel, pair_grad, out_weight):
    V = pltpu.VMEM
    dma = pltpu.SemaphoreType.DMA
    return pl.pallas_call(
        kernel,
        out_shape=[
            jax.ShapeDtypeStruct((8, 32, 32), F32),
            jax.ShapeDtypeStruct((16, 16, 32), F32),
            jax.ShapeDtypeStruct((1024, 128), F32),
        ],
        in_specs=[pl.BlockSpec(memory_space=pltpu.HBM)] * 4,
        out_specs=[pl.BlockSpec(memory_space=V)] * 3,
        scratch_shapes=[
            V((8, 32, 32), BF), V((16, 16, 32), BF), V((32, 16, 128), BF), V((1024, 128), BF),
            V((256, 32), F32), V((256, 32), F32), V((8, 1024), F32), V((16, 512), F32), V((512, 128), BF),
            V((32, 8, 1024), BF), V((16, 16, 512), BF), V((256, 1024), BF), V((256, 512), BF),
            V((512, 128), F32), V((4, 1024, 128), F32), V((1024, 512), BF), V((4, 1024, 128), F32),
            V((32, 8, 1024), BF), V((32, 8, 1024), BF), V((16, 16, 512), BF), V((16, 16, 512), BF),
            V((32, 32, 128), BF), V((32, 32, 128), BF), V((16, 32, 128), BF), V((32, 32, 128), BF),
            dma((4,)), dma((2, 32)), dma((2, 16)), dma((2, 32)), dma((2, 16)), dma((2, 32)), dma((2, 16)), dma((2, 32)),
        ],
        compiler_params=pltpu.CompilerParams(
            collective_id=0, has_side_effects=True, vmem_limit_bytes=48 << 20
        ),
        cost_estimate=pl.CostEstimate(flops=1 << 30, bytes_accessed=1 << 20, transcendentals=0),
        name="pair_backward",
    )(left_panel, right_panel, pair_grad, out_weight)


def solution(mesh):
    in_specs = (P("col", "row", None), P("row", "col", None), P("row", "col", None), P())
    out_specs = (P("col", "row", None), P("row", "col", None), P())
    return jax.shard_map(
        per_device, mesh=mesh, in_specs=in_specs, out_specs=out_specs, check_vma=False
    )
```

time: 291 us -> 91.2 us (0.31)
  waiting for transfers between devices: 92.3 us -> 0 us
  blocking collectives: 91.8 us -> 0 us
  Pallas kernels: 0 us -> 84.7 us
  starting transfers between devices: 44 us -> 0 us
  local copies, waits for them, and re-layouts: 44.3 us -> 5.63 us
  matrix products: 11.6 us -> 0 us
  other arithmetic: 3.13 us -> 0 us
    all_to_all x6 -> x0, waiting for transfers between devices: 92.3 us -> none  [the longest x3 48.7 us: summed_on_arrival(): blocks = lax.all_to_all(split_up(array, dim, peers), axis, 0, 0, tiled=True)]
    all_to_all x3 -> x0, blocking collectives: 91.8 us -> none  [the longest x2 55.6 us: summed_on_arrival(): blocks = lax.all_to_all(split_up(array, dim, peers), axis, 0, 0, tiled=True)]
    pallas_call x0 -> x1, Pallas kernels: none -> 84.7 us  [per_device(): pl.pallas_call(kernel, out_shape=[jax.ShapeDtypeStruct((8, 32, 32), F32),...]
    all_to_all x6 -> x0, starting transfers between devices: 44 us -> none  [the longest x3 28.3 us: from_everyone(): lax.all_to_all(jnp.broadcast_to(array[None], (peers, *array.shape)), axis...]
    reshape x15 -> x0, local copies, waits for them, and re-layouts: 29.2 us -> none  [the longest x4 7.6 us: advance(): expanded.reshape(block_rows, cols_here, channels, channels)]
    dot_general x10 -> x0, matrix products: 11.6 us -> none  [the longest x2 4.14 us: advance(): lax.dot_general(right_flat, expanded, (((1,), (1,)), ((), ())), preferred...]
    dynamic_slice x6 -> x0, local copies, waits for them, and re-layouts: 3.11 us -> none  [the longest x2 1.7 us: advance(): lax.dynamic_slice_in_dim(pair_grad, first_row, block_rows, 0)]
    unnamed x10 -> x11, local copies, waits for them, and re-layouts: 7.75 us -> 5.63 us
  transfers between devices with their start and end apart: 6 -> 0, of which waited for: 6 -> 0; matrix products, arithmetic and copies ran while one was open for 9% -> 0% of each run, Pallas kernels for 0% -> 0%
where the time goes in v1:
time: 91.2 us; the launch traced here: 91 us
  Pallas kernels  84.7 us (93%)
  local copies, waits for them, and re-layouts  5.63 us (6%)
    pallas_call x1, Pallas kernels, per_device(): pl.pallas_call(kernel, out_shape=[jax.ShapeDtypeStruct((8, 32, 32), F32),...  84.7 us
    unnamed x11, local copies, waits for them, and re-layouts  5.63 us

profile of v1, /device:TPU:1, one launch (start us, length us, event | category | flops | bytes accessed | tf_op | source)
XLA Modules:
  0.0 91.0 jit_solution(5349436502021360545)
XLA Ops:
  0.6 0.0 copy-start
  0.6 0.9 %copy-done = bf16[1024,128]{1,0:T(8,128)(2,1)S(1)} copy-done((bf16[1024,128]{1,0:T(8,128)(2,1)S(1)}, bf16[1024,128]{1,0:T(8,128)(2,1)}, u32[]{:S(2)}) %copy-start) | copy-done | bytes 262168
  1.6 0.0 copy-start.1
  1.6 0.9 copy-done.1
  2.5 0.0 copy-start.2
  2.5 0.8 copy-done.2
  3.3 0.0 copy-start.3
  3.3 0.8 copy-done.3
  4.2 84.7 %pair_backward.1 = (f32[8,32,32]{2,1,0:T(8,128)S(1)}, f32[16,16,32]{2,1,0:T(8,128)S(1)}, f32[1024,128]{1,0:T(8,128)S(1)}) custom-call(bf16[8,32,32]{2,1,0:T(8,128)(2,1)S(1)} %copy-done.2, bf16[16,16,32]{2,1,0:T(8,128)(2,1)S(1)} %copy-done.3, bf16[32,16,128]{2,1,0:T(8,128)(2,1)S(1)} %copy-done.1, bf16[1024,128]{1,0:T(8,128)(2,1)S(1)} %copy-done), custom_call_target="tpu_custom_call" | custom-call | flops 1073741824 | bytes 1048576 | tf_op jit(solution)/shard_map/pair_backward/pallas_call | solution.py:251
  88.9 0.7 copy.10
  89.5 0.7 copy.11
  90.2 0.8 copy.12
Async XLA Ops:
  0.6 1.0 %copy-start = (bf16[1024,128]{1,0:T(8,128)(2,1)S(1)}, bf16[1024,128]{1,0:T(8,128)(2,1)}, u32[]{:S(2)}) copy-start(bf16[1024,128]{1,0:T(8,128)(2,1)} %w_hbm.1) | copy-start | bytes 786436
  1.6 0.9 copy-start.1
  2.5 0.8 copy-start.2
  3.3 0.8 copy-start.3

commit v2 on v1

v2 whole, which is shorter than its diff:
```python
import jax
import jax.numpy as jnp
from jax import lax
from jax.experimental import pallas as pl
from jax.experimental.pallas import tpu as pltpu
from jax.sharding import PartitionSpec as P

MESH = pl.DeviceIdType.MESH
F32, BF = jnp.float32, jnp.bfloat16
ROWS, ZS, XL = 16, 16, 2
COLS = ZS * XL
PLANE = ROWS * XL
NEAR = ((2, 0), (2, 1), (1, 1), (-1, 1), (1, 0), (-1, 0), (0, 1))
GREETED = len(NEAR) + 2 + (ROWS - 1) + (ROWS - 1)


def swap4(x):
    lane = lax.broadcasted_iota(jnp.int32, x[0].shape, 1)
    low = lane < 64
    even = (lane // 32) % 2 == 0
    r = [pltpu.roll(v, 64, 1) for v in x]
    a = [
        jnp.where(low, x[0], r[2]),
        jnp.where(low, x[1], r[3]),
        jnp.where(low, r[0], x[2]),
        jnp.where(low, r[1], x[3]),
    ]
    y = []
    for p in (0, 2):
        y.append(jnp.where(even, a[p], pltpu.roll(a[p + 1], 32, 1)))
        y.append(jnp.where(even, pltpu.roll(a[p], 96, 1), a[p + 1]))
    return y


def expand(gji, w, eb):
    wd = 256

    def part(a, _):
        w_rows = w[pl.ds(pl.multiple_of(a * wd, wd), wd), :]
        m = lax.dot_general(gji[...], w_rows, (((1,), (1,)), ((), ())), preferred_element_type=F32)
        m = (m * (1.0 / 256)).astype(BF)
        for h in range(wd // 128):
            for jg in range(4):
                for i0 in range(2):
                    x = []
                    for b in range(4):
                        r0 = (4 * jg + b) * 32 + 16 * i0
                        x.append(m[r0 : r0 + 16, 128 * h : 128 * h + 128])
                    y = swap4(x)
                    for q in range(4):
                        r0 = pl.multiple_of(a * wd + h * 128 + q * 32 + 16 * i0, 16)
                        eb[pl.ds(r0, 16), 128 * jg : 128 * jg + 128] = y[q]
        return 0

    lax.fori_loop(0, 1024 // wd, part, 0, unroll=4)


def left_term(rg, eb, out):
    wd = 256

    def part(t, _):
        rows = pl.ds(pl.multiple_of(t * wd, wd), wd)
        v = lax.dot_general(rg[...], eb[rows, :], (((1,), (1,)), ((), ())), preferred_element_type=F32)
        for m in range(4):
            out[:, :, m, :, rows] = v[64 * m : 64 * m + 64].reshape(4, 2, 8, wd).astype(BF)
        return 0

    lax.fori_loop(0, 1024 // wd, part, 0, unroll=4)


def right_term(lg, eb, out):
    wd = 256

    def part(t, _):
        cols = pl.ds(pl.multiple_of(t * wd, wd), wd)
        v = jnp.dot(lg[...], eb[:, cols], preferred_element_type=F32)
        out[:, :, cols] = v.reshape(16, 16, wd).astype(BF)
        return 0

    lax.fori_loop(0, 512 // wd, part, 0, unroll=2)


def outer_weight(half, lg, rg, gt, out):
    wd = 512
    o = lax.dot_general(
        lg[:, half * wd : half * wd + wd], rg[...], (((0,), (0,)), ((), ())), preferred_element_type=F32
    )
    o = (o * (1.0 / 256)).astype(BF)
    tiles = []
    for h in range(wd // 128):
        parts = [[None] * 2 for _ in range(16)]
        for jg in range(4):
            for i0 in range(2):
                x = []
                for q in range(4):
                    r0 = h * 128 + q * 32 + 16 * i0
                    x.append(o[r0 : r0 + 16, 128 * jg : 128 * jg + 128])
                y = swap4(x)
                for b in range(4):
                    parts[4 * jg + b][i0] = y[b]
        tiles.append(jnp.concatenate([p for q in parts for p in q], axis=0))
    v = jnp.dot(gt[...], jnp.concatenate(tiles, axis=1), preferred_element_type=F32).T
    out[half * 16 : half * 16 + 16] = v.reshape(16, 32, 128).astype(BF)


def kernel(
    l_hbm, r_hbm, g_hbm, w_hbm, lo, ro, wo,
    lv, rv, gv, wv, lf, rf, gf, lflat, rflat, gji, gt,
    lb, rb, lg, rg, eb,
    sl, ra, sa, sb, rl, sr, rr, sw, rw, zb, ab,
    in_sem, ag_l, ag_r, rs_a, rs_b, rs_r, rs_w, z_w, ag_w,
):
    row, col = lax.axis_index("row"), lax.axis_index("col")
    z, xl = col // XL, col % XL
    plane = xl * ROWS + row

    def at_zx(dz, dx):
        c = ((z + dz) % ZS) * XL + (xl + dx) % XL
        return {"row": row, "col": c}

    def row_at(k):
        r = (row + k) % ROWS
        return {"row": r, "col": col}, r

    def plane_at(k):
        r, x = (row + k % ROWS) % ROWS, (xl + k // ROWS) % XL
        return {"row": r, "col": z * XL + x}, x * ROWS + r

    def z_at(k):
        zz = (z + k) % ZS
        return {"row": row, "col": zz * XL + xl}, zz

    inputs = [
        pltpu.make_async_copy(src, dst, in_sem.at[n])
        for n, (src, dst) in enumerate(((l_hbm, lv), (r_hbm, rv), (g_hbm, gv), (w_hbm, wv)))
    ]
    for c in inputs:
        c.start()

    barrier = pltpu.get_barrier_semaphore()

    def greet(device):
        pl.semaphore_signal(barrier, inc=1, device_id=device, device_id_type=MESH)

    def greet_all(at, first, last):
        def one(k, _):
            greet(at(k)[0])
            return 0

        lax.fori_loop(first, last, one, 0)

    greet(at_zx(4, 0))
    greet(at_zx(-4, 0))
    greet_all(row_at, 1, ROWS)
    for dz, dx in NEAR:
        greet(at_zx(-dz, dx))
    greet_all(plane_at, ROWS + 1, PLANE)

    inputs[0].wait()
    inputs[1].wait()
    lf[...] = jnp.swapaxes(lv[...].astype(F32), 1, 2).reshape(256, 32)
    rf[...] = rv[...].reshape(256, 32).astype(F32)
    for i in range(32):
        lflat[:, 32 * i : 32 * i + 32] = lf[pl.ds(i, 8, stride=32), :]
    for j in range(16):
        rflat[:, 32 * j : 32 * j + 32] = rf[pl.ds(j, 16, stride=16), :]
    lb[col] = lflat[...].astype(BF)
    rb[row] = rflat[...].astype(BF)

    pl.semaphore_wait(barrier, GREETED)

    def left_copy(d, dz, dx):
        slot = ((z + ZS - d) % ZS) * XL + xl
        k = ((d + dz) % ZS) * XL + dx
        return pltpu.make_async_remote_copy(
            src_ref=lb.at[slot],
            dst_ref=lb.at[slot],
            send_sem=ag_l.at[0, k],
            recv_sem=ag_l.at[1, k],
            device_id=at_zx(dz, dx),
            device_id_type=MESH,
        )

    def left_arrived(k, wait):
        slot = ((z + ZS - k // XL) % ZS) * XL + (xl + k % XL) % XL
        c = pltpu.make_async_remote_copy(
            src_ref=lb.at[slot],
            dst_ref=lb.at[slot],
            send_sem=ag_l.at[0, k],
            recv_sem=ag_l.at[1, k],
            device_id=at_zx(0, 1),
            device_id_type=MESH,
        )
        wait(c)

    def spread(d):
        for dz, dx in NEAR:
            left_copy(d, dz, dx).start()

    def copies(at, n, src_slot, dst_slot, sems):
        def make(k):
            where, slot = at(k)
            return pltpu.make_async_remote_copy(
                src_ref=src_slot(slot),
                dst_ref=dst_slot,
                send_sem=sems.at[0, k],
                recv_sem=sems.at[1, k],
                device_id=where,
                device_id_type=MESH,
            )

        def each(act, first, last):
            def one(k, _):
                act(make(k))
                return 0

            lax.fori_loop(first, last, one, 0)

        return (
            lambda first=1, last=n: each(lambda c: c.start(), first, last),
            lambda: each(lambda c: c.wait_recv(), 1, n),
            lambda: each(lambda c: c.wait_send(), 1, n),
        )

    ag_r_start, ag_r_recv, ag_r_sent = copies(row_at, ROWS, lambda s: rb.at[row], rb.at[row], ag_r)
    rs_r_start, rs_r_recv, rs_r_sent = copies(row_at, ROWS, lambda s: sr.at[s], rr.at[row], rs_r)
    rs_w_start, rs_w_recv, rs_w_sent = copies(plane_at, PLANE, lambda s: sw.at[s], rw.at[plane], rs_w)
    z_w_start, z_w_recv, z_w_sent = copies(z_at, ZS, lambda s: zb.at[z], zb.at[z], z_w)
    ag_w_start, ag_w_recv, ag_w_sent = copies(plane_at, PLANE, lambda s: ab.at[plane], ab.at[plane], ag_w)

    left_copy(0, 4, 0).start()
    left_copy(0, -4, 0).start()
    ag_r_start()
    spread(0)

    inputs[2].wait()
    inputs[3].wait()
    gf[...] = gv[...].reshape(512, 128).astype(F32)
    for j in range(16):
        gji[32 * j : 32 * j + 32, :] = gf[pl.ds(j, 32, stride=16), :].astype(BF)
    gt[...] = gji[...].T
    expand(gji, wv, eb)

    left_arrived(4 * XL, lambda c: c.wait_recv())
    left_copy(4, 4, 0).start()
    spread(4)
    left_arrived(12 * XL, lambda c: c.wait_recv())
    spread(12)
    ag_r_recv()
    rg[...] = rb[...].reshape(256, 512)
    left_term(rg, eb, sl)
    left_arrived(8 * XL, lambda c: c.wait_recv())
    spread(8)

    zr, zq = z % 4, z // 4

    def group_copy(n):
        dz, dx = NEAR[n]
        return pltpu.make_async_remote_copy(
            src_ref=sl.at[(z + dz) % 4, (xl + dx) % XL],
            dst_ref=ra.at[n],
            send_sem=rs_a.at[0, n],
            recv_sem=rs_a.at[1, n],
            device_id=at_zx(dz, dx),
            device_id_type=MESH,
        )

    for n in range(len(NEAR)):
        group_copy(n).start()

    def rest(act):
        def one(k, _):
            left_arrived(k, act)
            return 0

        lax.fori_loop(1, 8, one, 0)
        lax.fori_loop(9, 16, one, 0)
        lax.fori_loop(17, 24, one, 0)
        lax.fori_loop(25, 32, one, 0)

    rest(lambda c: c.wait_recv())
    lg[...] = lb[...].astype(F32).reshape(256, 1024).astype(BF)
    for half in range(2):
        outer_weight(half, lg, rg, gt, sw)
        away = (xl + half) % XL
        rs_w_start(away * ROWS + (1 - away), away * ROWS + ROWS)
    rw[plane] = sw[plane]
    right_term(lg, eb, sr)
    rs_r_start()
    rr[row] = sr[row]

    for n in range(len(NEAR)):
        group_copy(n).wait_recv()
    v = sl[zr, xl].astype(F32)
    for n in range(len(NEAR)):
        v = v + ra[n].astype(F32)
    sa[...] = v
    sb[...] = v.astype(BF)

    def far_copy(q):
        return pltpu.make_async_remote_copy(
            src_ref=sb.at[(zq + q) % 4],
            dst_ref=rl.at[q - 1],
            send_sem=rs_b.at[0, q],
            recv_sem=rs_b.at[1, q],
            device_id=at_zx(4 * q, 0),
            device_id_type=MESH,
        )

    for q in (2, 1, 3):
        far_copy(q).start()

    rs_w_recv()
    zb[z] = jnp.sum(rw[...].astype(F32), axis=0).astype(BF)
    z_w_start()
    rs_r_recv()
    rflat[...] = jnp.sum(rr[...].astype(F32), axis=0)
    for j in range(16):
        ro[:, j, :] = rflat[:, 32 * j : 32 * j + 32]
    z_w_recv()
    ab[plane] = jnp.sum(zb[...].astype(F32), axis=0).astype(BF)
    ag_w_start()
    for q in (1, 2, 3):
        far_copy(q).wait_recv()
    lflat[...] = sa[zq] + rl[0].astype(F32) + rl[1].astype(F32) + rl[2].astype(F32)
    for i in range(32):
        lf[pl.ds(i, 8, stride=32), :] = lflat[:, 32 * i : 32 * i + 32]
    lo[...] = jnp.swapaxes(lf[...].reshape(8, 32, 32), 1, 2)
    ag_w_recv()
    wo[...] = ab[...].astype(F32).reshape(1024, 128) * (1.0 / 512)

    for done in (ag_r_sent, rs_r_sent, rs_w_sent, z_w_sent, ag_w_sent):
        done()
    rest(lambda c: c.wait_send())
    for d in (4, 8, 12):
        left_arrived(d * XL, lambda c: c.wait_send())
    for n in range(len(NEAR)):
        group_copy(n).wait_send()
    for q in (1, 2, 3):
        far_copy(q).wait_send()


def per_device(left_panel, right_panel, pair_grad, out_weight):
    V = pltpu.VMEM
    dma = pltpu.SemaphoreType.DMA
    return pl.pallas_call(
        kernel,
        out_shape=[
            jax.ShapeDtypeStruct((8, 32, 32), F32),
            jax.ShapeDtypeStruct((16, 16, 32), F32),
            jax.ShapeDtypeStruct((1024, 128), F32),
        ],
        in_specs=[pl.BlockSpec(memory_space=pltpu.HBM)] * 4,
        out_specs=[pl.BlockSpec(memory_space=V)] * 3,
        scratch_shapes=[
            V((8, 32, 32), BF), V((16, 16, 32), BF), V((32, 16, 128), BF), V((1024, 128), BF),
            V((256, 32), F32), V((256, 32), F32), V((512, 128), F32),
            V((8, 1024), F32), V((16, 512), F32), V((512, 128), BF), V((128, 512), BF),
            V((32, 8, 1024), BF), V((16, 16, 512), BF), V((256, 1024), BF), V((256, 512), BF), V((1024, 512), BF),
            V((4, 2, 4, 8, 1024), BF), V((7, 4, 8, 1024), BF), V((4, 8, 1024), F32), V((4, 8, 1024), BF), V((3, 8, 1024), BF),
            V((16, 16, 512), BF), V((16, 16, 512), BF),
            V((32, 32, 128), BF), V((32, 32, 128), BF), V((16, 32, 128), BF), V((32, 32, 128), BF),
            dma((4,)), dma((2, 32)), dma((2, 16)), dma((2, 7)), dma((2, 4)), dma((2, 16)), dma((2, 32)), dma((2, 16)), dma((2, 32)),
        ],
        compiler_params=pltpu.CompilerParams(
            collective_id=0, has_side_effects=True, vmem_limit_bytes=60 << 20
        ),
        cost_estimate=pl.CostEstimate(flops=1 << 30, bytes_accessed=1 << 20, transcendentals=0),
        name="pair_backward",
    )(left_panel, right_panel, pair_grad, out_weight)


def solution(mesh):
    in_specs = (P("col", "row", None), P("row", "col", None), P("row", "col", None), P())
    out_specs = (P("col", "row", None), P("row", "col", None), P())
    return jax.shard_map(
        per_device, mesh=mesh, in_specs=in_specs, out_specs=out_specs, check_vma=False
    )
```

time: 91.2 us -> 66.3 us (0.73)
  Pallas kernels: 84.7 us -> 61.5 us
  local copies, waits for them, and re-layouts: 5.63 us -> 3.99 us
    pallas_call x1, Pallas kernels: 84.7 us -> 61.5 us  [per_device(): pl.pallas_call(kernel, out_shape=[jax.ShapeDtypeStruct((8, 32, 32), F32),...]
    unnamed x11 -> x5, local copies, waits for them, and re-layouts: 5.63 us -> 3.99 us
where the time goes in v2:
time: 66.3 us; the launch traced here: 66.1 us
  Pallas kernels  61.5 us (93%)
  local copies, waits for them, and re-layouts  3.99 us (6%)
    pallas_call x1, Pallas kernels, per_device(): pl.pallas_call(kernel, out_shape=[jax.ShapeDtypeStruct((8, 32, 32), F32),...  61.5 us
    unnamed x5, local copies, waits for them, and re-layouts  3.99 us

profile of v2, /device:TPU:1, one launch (start us, length us, event | category | flops | bytes accessed | tf_op | source)
XLA Modules:
  0.0 66.1 jit_solution(8984780277194552176)
XLA Ops:
  0.6 61.5 %pair_backward.1 = (f32[8,32,32]{2,1,0:T(8,128)}, f32[16,16,32]{2,1,0:T(8,128)}, f32[1024,128]{1,0:T(8,128)}) custom-call(bf16[8,32,32]{2,1,0:T(8,128)(2,1)} %l_hbm.1, bf16[16,16,32]{2,1,0:T(8,128)(2,1)} %r_hbm.1, bf16[32,16,128]{2,1,0:T(8,128)(2,1)} %g_hbm.1, bf16[1024,128]{1,0:T(8,128)(2,1)} %w_hbm.1), custom_call_target="tpu_custom_call" | custom-call | flops 1073741824 | bytes 1048576 | tf_op jit(solution)/shard_map/pair_backward/pallas_call | solution.py:346
  62.1 0.0 copy-start
  62.1 1.6 %copy.10 = f32[8,32,32]{2,1,0:T(8,128)} copy(f32[8,32,32]{2,1,0:T(8,128)} %get-tuple-element.6) | data formatting | bytes 65536
  63.8 1.6 %copy.11 = f32[16,16,32]{2,1,0:T(8,128)} copy(f32[16,16,32]{2,1,0:T(8,128)} %get-tuple-element.7) | data formatting | bytes 65536
  65.3 0.0 copy-done
  65.3 0.8 %copy.12 = f32[1024,128]{1,0:T(8,128)} copy(f32[1024,128]{1,0:T(8,128)S(1)} %copy-done) | data formatting | bytes 1048576
Async XLA Ops:
  62.1 3.2 %copy-start = (f32[1024,128]{1,0:T(8,128)S(1)}, f32[1024,128]{1,0:T(8,128)}, u32[]{:S(2)}) copy-start(f32[1024,128]{1,0:T(8,128)} %get-tuple-element.8) | copy-start | bytes 1572868

commit v3 on v2

--- a/solution.py
+++ b/solution.py
@@ -11,7 +11,7 @@
 COLS = ZS * XL
 PLANE = ROWS * XL
 NEAR = ((2, 0), (2, 1), (1, 1), (-1, 1), (1, 0), (-1, 0), (0, 1))
-GREETED = len(NEAR) + 2 + (ROWS - 1) + (ROWS - 1)
+GREETED = len(NEAR) + 2 + (ROWS - 1)
 
 
 def swap4(x):
@@ -83,7 +83,7 @@
 def outer_weight(half, lg, rg, gt, out):
     wd = 512
     o = lax.dot_general(
-        lg[:, half * wd : half * wd + wd], rg[...], (((0,), (0,)), ((), ())), preferred_element_type=F32
+        lg[:, pl.ds(pl.multiple_of(half * wd, wd), wd)], rg[...], (((0,), (0,)), ((), ())), preferred_element_type=F32
     )
     o = (o * (1.0 / 256)).astype(BF)
     tiles = []
@@ -100,7 +100,7 @@
                     parts[4 * jg + b][i0] = y[b]
         tiles.append(jnp.concatenate([p for q in parts for p in q], axis=0))
     v = jnp.dot(gt[...], jnp.concatenate(tiles, axis=1), preferred_element_type=F32).T
-    out[half * 16 : half * 16 + 16] = v.reshape(16, 32, 128).astype(BF)
+    out[pl.ds(half * 16, 16)] = v.reshape(16, 32, 128).astype(BF)
 
 
 def kernel(
@@ -127,7 +127,7 @@
         return {"row": r, "col": z * XL + x}, x * ROWS + r
 
     def z_at(k):
-        zz = (z + k) % ZS
+        zz = (z + ZS // 2 + k // 2 * (1 - 2 * (1 - k % 2))) % ZS
         return {"row": row, "col": zz * XL + xl}, zz
 
     inputs = [
@@ -154,7 +154,6 @@
     greet_all(row_at, 1, ROWS)
     for dz, dx in NEAR:
         greet(at_zx(-dz, dx))
-    greet_all(plane_at, ROWS + 1, PLANE)
 
     inputs[0].wait()
     inputs[1].wait()
@@ -246,11 +245,11 @@
     spread(4)
     left_arrived(12 * XL, lambda c: c.wait_recv())
     spread(12)
+    left_arrived(8 * XL, lambda c: c.wait_recv())
+    spread(8)
     ag_r_recv()
     rg[...] = rb[...].reshape(256, 512)
     left_term(rg, eb, sl)
-    left_arrived(8 * XL, lambda c: c.wait_recv())
-    spread(8)
 
     zr, zq = z % 4, z // 4
 
@@ -280,10 +279,10 @@
 
     rest(lambda c: c.wait_recv())
     lg[...] = lb[...].astype(F32).reshape(256, 1024).astype(BF)
-    for half in range(2):
-        outer_weight(half, lg, rg, gt, sw)
-        away = (xl + half) % XL
-        rs_w_start(away * ROWS + (1 - away), away * ROWS + ROWS)
+    outer_weight(1 - xl, lg, rg, gt, sw)
+    rs_w_start(ROWS, PLANE)
+    outer_weight(xl, lg, rg, gt, sw)
+    rs_w_start(1, ROWS)
     rw[plane] = sw[plane]
     right_term(lg, eb, sr)
     rs_r_start()
@@ -340,10 +339,19 @@
         far_copy(q).wait_send()
 
 
+def hand_over(l, r, w, lo, ro, wo, sem):
+    moves = [pltpu.make_async_copy(a, b, sem.at[n]) for n, (a, b) in enumerate(((w, wo), (l, lo), (r, ro)))]
+    for m in moves:
+        m.start()
+    for m in moves:
+        m.wait()
+
+
 def per_device(left_panel, right_panel, pair_grad, out_weight):
     V = pltpu.VMEM
     dma = pltpu.SemaphoreType.DMA
-    return pl.pallas_call(
+    args = [pltpu.with_memory_space_constraint(a, pltpu.HBM) for a in (left_panel, right_panel, pair_grad, out_weight)]
+    raw = pl.pallas_call(
         kernel,
         out_shape=[
             jax.ShapeDtypeStruct((8, 32, 32), F32),
@@ -363,11 +371,20 @@
             dma((4,)), dma((2, 32)), dma((2, 16)), dma((2, 7)), dma((2, 4)), dma((2, 16)), dma((2, 32)), dma((2, 16)), dma((2, 32)),
         ],
         compiler_params=pltpu.CompilerParams(
-            collective_id=0, has_side_effects=True, vmem_limit_bytes=60 << 20
+            collective_id=0, has_side_effects=True, vmem_limit_bytes=24 << 20
         ),
         cost_estimate=pl.CostEstimate(flops=1 << 30, bytes_accessed=1 << 20, transcendentals=0),
         name="pair_backward",
-    )(left_panel, right_panel, pair_grad, out_weight)
+    )(*args)
+    shapes = [jax.ShapeDtypeStruct(a.shape, a.dtype) for a in raw]
+    return pl.pallas_call(
+        hand_over,
+        out_shape=shapes,
+        in_specs=[pl.BlockSpec(memory_space=V)] * 3,
+        out_specs=[pl.BlockSpec(memory_space=pltpu.HBM)] * 3,
+        scratch_shapes=[dma((3,))],
+        name="hand_over",
+    )(*[pltpu.with_memory_space_constraint(a, V) for a in raw])
 
 
 def solution(mesh):

time: 66.3 us -> 61.2 us (0.923)
  local copies, waits for them, and re-layouts: 3.99 us -> 0 us
  Pallas kernels: 61.5 us -> 60.4 us
    unnamed x5 -> x0, local copies, waits for them, and re-layouts: 3.99 us -> none
    pallas_call x1, Pallas kernels: 61.5 us -> 59.5 us  [per_device(): pl.pallas_call(kernel, out_shape=[jax.ShapeDtypeStruct((8, 32, 32), F32),...]
    pallas_call x0 -> x1, Pallas kernels: none -> 0.9 us  [per_device(): pl.pallas_call(hand_over, out_shape=shapes, in_specs=[pl.BlockSpec(memory...]
where the time goes in v3:
time: 61.2 us; the launch traced here: 61 us
  Pallas kernels  60.4 us (99%)
  between operations  0.64 us (1%)
    pallas_call x1, Pallas kernels, per_device(): pl.pallas_call(kernel, out_shape=[jax.ShapeDtypeStruct((8, 32, 32), F32),...  59.5 us

profile of v3, /device:TPU:1, one launch (start us, length us, event | category | flops | bytes accessed | tf_op | source)
XLA Modules:
  0.0 61.0 jit_solution(1441830220018042839)
XLA Ops:
  0.6 59.5 %pair_backward.1 = (f32[8,32,32]{2,1,0:T(8,128)S(1)}, f32[16,16,32]{2,1,0:T(8,128)S(1)}, f32[1024,128]{1,0:T(8,128)S(1)}) custom-call(bf16[8,32,32]{2,1,0:T(8,128)(2,1)} %l_hbm.1, bf16[16,16,32]{2,1,0:T(8,128)(2,1)} %r_hbm.1, bf16[32,16,128]{2,1,0:T(8,128)(2,1)} %g_hbm.1, bf16[1024,128]{1,0:T(8,128)(2,1)} %w_hbm.1), custom_call_target="tpu_custom_call" | custom-call | flops 1073741824 | bytes 1048576 | tf_op jit(solution)/shard_map/pair_backward/pallas_call | solution.py:354
  60.1 0.9 %hand_over.1 = (f32[8,32,32]{2,1,0:T(8,128)}, f32[16,16,32]{2,1,0:T(8,128)}, f32[1024,128]{1,0:T(8,128)}) custom-call(f32[8,32,32]{2,1,0:T(8,128)S(1)} %get-tuple-element.6.l, f32[16,16,32]{2,1,0:T(8,128)S(1)} %get-tuple-element.7.r, f32[1024,128]{1,0:T(8,128)S(1)} %get-tuple-element.8.w), custom_call_target="tpu_custom_call" | custom-call | tf_op jit(solution)/shard_map/hand_over/pallas_call | solution.py:380

commit v4 on v3

--- a/solution.py
+++ b/solution.py
@@ -9,9 +9,13 @@
 F32, BF = jnp.float32, jnp.bfloat16
 ROWS, ZS, XL = 16, 16, 2
 COLS = ZS * XL
-PLANE = ROWS * XL
-NEAR = ((2, 0), (2, 1), (1, 1), (-1, 1), (1, 0), (-1, 0), (0, 1))
-GREETED = len(NEAR) + 2 + (ROWS - 1)
+CHIPS = 16
+NEAR = ((2, 1), (-2, 1), (2, 0), (-2, 0), (1, 1), (-1, 1), (1, 0), (-1, 0), (0, 1))
+FAR = 5
+LAST = ((3, 1), (3, 0))
+GREETED = len(NEAR) + 2 + len(LAST) + (ROWS - 1)
+GROUP = ((2, 1), (2, 0), (1, 1), (-1, 1), (1, 0), (-1, 0), (0, 1))
+ACROSS = (6, 5, 7, 10, 14, 2, 4, 9, 11, 13, 15, 1, 3, 8, 12)
 
 
 def swap4(x):
@@ -80,7 +84,7 @@
     lax.fori_loop(0, 512 // wd, part, 0, unroll=2)
 
 
-def outer_weight(half, lg, rg, gt, out):
+def outer_weight(half, lg, rg, gt):
     wd = 512
     o = lax.dot_general(
         lg[:, pl.ds(pl.multiple_of(half * wd, wd), wd)], rg[...], (((0,), (0,)), ((), ())), preferred_element_type=F32
@@ -100,19 +104,21 @@
                     parts[4 * jg + b][i0] = y[b]
         tiles.append(jnp.concatenate([p for q in parts for p in q], axis=0))
     v = jnp.dot(gt[...], jnp.concatenate(tiles, axis=1), preferred_element_type=F32).T
-    out[pl.ds(half * 16, 16)] = v.reshape(16, 32, 128).astype(BF)
+    return v.reshape(16, 32, 128)
 
 
 def kernel(
     l_hbm, r_hbm, g_hbm, w_hbm, lo, ro, wo,
     lv, rv, gv, wv, lf, rf, gf, lflat, rflat, gji, gt,
     lb, rb, lg, rg, eb,
-    sl, ra, sa, sb, rl, sr, rr, sw, rw, zb, ab,
-    in_sem, ag_l, ag_r, rs_a, rs_b, rs_r, rs_w, z_w, ag_w,
+    sl, ra, sa, sb, rl, sr, rr, wp, wq, sw, rw, zb, ab,
+    in_sem, ag_l, ag_r, rs_a, rs_b, rs_r, c_w, rs_w, z_w, ag_w, f_w,
 ):
     row, col = lax.axis_index("row"), lax.axis_index("col")
     z, xl = col // XL, col % XL
-    plane = xl * ROWS + row
+    xh, y, core = row // 8, (row // 2) % 4, row % 2
+    chip = xl * 8 + row // 2
+    partner = {"row": row + 1 - 2 * core, "col": col}
 
     def at_zx(dz, dx):
         c = ((z + dz) % ZS) * XL + (xl + dx) % XL
@@ -122,9 +128,9 @@
         r = (row + k) % ROWS
         return {"row": r, "col": col}, r
 
-    def plane_at(k):
-        r, x = (row + k % ROWS) % ROWS, (xl + k // ROWS) % XL
-        return {"row": r, "col": z * XL + x}, x * ROWS + r
+    def chip_at(k, sign):
+        r, x = ((xh + k // 4) % 2) * 4 + (y + sign * k) % 4, (xl + k // 8) % XL
+        return {"row": r * 2 + core, "col": z * XL + x}, x * 8 + r
 
     def z_at(k):
         zz = (z + ZS // 2 + k // 2 * (1 - 2 * (1 - k % 2))) % ZS
@@ -149,10 +155,10 @@
 
         lax.fori_loop(first, last, one, 0)
 
-    greet(at_zx(4, 0))
-    greet(at_zx(-4, 0))
+    greet(at_zx(FAR, 0))
+    greet(at_zx(-FAR, 0))
     greet_all(row_at, 1, ROWS)
-    for dz, dx in NEAR:
+    for dz, dx in LAST + NEAR:
         greet(at_zx(-dz, dx))
 
     inputs[0].wait()
@@ -223,12 +229,10 @@
 
     ag_r_start, ag_r_recv, ag_r_sent = copies(row_at, ROWS, lambda s: rb.at[row], rb.at[row], ag_r)
     rs_r_start, rs_r_recv, rs_r_sent = copies(row_at, ROWS, lambda s: sr.at[s], rr.at[row], rs_r)
-    rs_w_start, rs_w_recv, rs_w_sent = copies(plane_at, PLANE, lambda s: sw.at[s], rw.at[plane], rs_w)
     z_w_start, z_w_recv, z_w_sent = copies(z_at, ZS, lambda s: zb.at[z], zb.at[z], z_w)
-    ag_w_start, ag_w_recv, ag_w_sent = copies(plane_at, PLANE, lambda s: ab.at[plane], ab.at[plane], ag_w)
-
-    left_copy(0, 4, 0).start()
-    left_copy(0, -4, 0).start()
+
+    left_copy(0, FAR, 0).start()
+    left_copy(0, -FAR, 0).start()
     ag_r_start()
     spread(0)
 
@@ -240,13 +244,12 @@
     gt[...] = gji[...].T
     expand(gji, wv, eb)
 
-    left_arrived(4 * XL, lambda c: c.wait_recv())
-    left_copy(4, 4, 0).start()
-    spread(4)
-    left_arrived(12 * XL, lambda c: c.wait_recv())
-    spread(12)
-    left_arrived(8 * XL, lambda c: c.wait_recv())
-    spread(8)
+    left_arrived(FAR * XL, lambda c: c.wait_recv())
+    for dz, dx in LAST:
+        left_copy(FAR, dz, dx).start()
+    spread(FAR)
+    left_arrived((ZS - FAR) * XL, lambda c: c.wait_recv())
+    spread(ZS - FAR)
     ag_r_recv()
     rg[...] = rb[...].reshape(256, 512)
     left_term(rg, eb, sl)
@@ -254,7 +257,7 @@
     zr, zq = z % 4, z // 4
 
     def group_copy(n):
-        dz, dx = NEAR[n]
+        dz, dx = GROUP[n]
         return pltpu.make_async_remote_copy(
             src_ref=sl.at[(z + dz) % 4, (xl + dx) % XL],
             dst_ref=ra.at[n],
@@ -264,34 +267,75 @@
             device_id_type=MESH,
         )
 
-    for n in range(len(NEAR)):
-        group_copy(n).start()
-
     def rest(act):
         def one(k, _):
             left_arrived(k, act)
             return 0
 
-        lax.fori_loop(1, 8, one, 0)
-        lax.fori_loop(9, 16, one, 0)
-        lax.fori_loop(17, 24, one, 0)
-        lax.fori_loop(25, 32, one, 0)
+        lax.fori_loop(1, FAR * XL, one, 0)
+        lax.fori_loop(FAR * XL + 1, (ZS - FAR) * XL, one, 0)
+        lax.fori_loop((ZS - FAR) * XL + 1, COLS, one, 0)
 
     rest(lambda c: c.wait_recv())
+    for n in range(len(GROUP)):
+        group_copy(n).start()
     lg[...] = lb[...].astype(F32).reshape(256, 1024).astype(BF)
-    outer_weight(1 - xl, lg, rg, gt, sw)
-    rs_w_start(ROWS, PLANE)
-    outer_weight(xl, lg, rg, gt, sw)
-    rs_w_start(1, ROWS)
-    rw[plane] = sw[plane]
+    halves = pltpu.make_async_remote_copy(
+        src_ref=wp, dst_ref=wq, send_sem=c_w.at[0], recv_sem=c_w.at[1], device_id=partner, device_id_type=MESH
+    )
+    wp[...] = outer_weight(1 - core, lg, rg, gt)
+    halves.start()
+    own_half = outer_weight(core, lg, rg, gt)
+    halves.wait_recv()
+    sw[...] = (own_half + wq[...]).astype(BF)
+
+    def share_copy(k):
+        where, slot = chip_at(k, 1)
+        return pltpu.make_async_remote_copy(
+            src_ref=sw.at[slot],
+            dst_ref=rw.at[chip],
+            send_sem=rs_w.at[0, k],
+            recv_sem=rs_w.at[1, k],
+            device_id=where,
+            device_id_type=MESH,
+        )
+
+    def back_copy(k):
+        return pltpu.make_async_remote_copy(
+            src_ref=ab.at[core, chip],
+            dst_ref=ab.at[core, chip],
+            send_sem=ag_w.at[0, k],
+            recv_sem=ag_w.at[1, k],
+            device_id=chip_at(k, 1)[0],
+            device_id_type=MESH,
+        )
+
+    def pass_on(k):
+        slot = chip_at(k, -1)[1]
+        return pltpu.make_async_remote_copy(
+            src_ref=ab.at[core, slot],
+            dst_ref=ab.at[core, slot],
+            send_sem=f_w.at[0, k],
+            recv_sem=f_w.at[1, k],
+            device_id=partner,
+            device_id_type=MESH,
+        )
+
+    for k in ACROSS:
+        share_copy(k).start()
+    rw[chip] = sw[chip]
     right_term(lg, eb, sr)
+    rr[row] = sr[row]
+    for k in ACROSS:
+        share_copy(k).wait_recv()
+    zb[z] = jnp.sum(rw[...].astype(F32), axis=0).astype(BF)
+    z_w_start()
     rs_r_start()
-    rr[row] = sr[row]
-
-    for n in range(len(NEAR)):
+
+    for n in range(len(GROUP)):
         group_copy(n).wait_recv()
     v = sl[zr, xl].astype(F32)
-    for n in range(len(NEAR)):
+    for n in range(len(GROUP)):
         v = v + ra[n].astype(F32)
     sa[...] = v
     sb[...] = v.astype(BF)
@@ -309,31 +353,40 @@
     for q in (2, 1, 3):
         far_copy(q).start()
 
-    rs_w_recv()
-    zb[z] = jnp.sum(rw[...].astype(F32), axis=0).astype(BF)
-    z_w_start()
+    z_w_recv()
+    ab[core, chip] = jnp.sum(zb[...].astype(F32), axis=0).astype(BF)
+    for k in ACROSS:
+        back_copy(k).start()
+    pass_on(0).start()
     rs_r_recv()
     rflat[...] = jnp.sum(rr[...].astype(F32), axis=0)
     for j in range(16):
         ro[:, j, :] = rflat[:, 32 * j : 32 * j + 32]
-    z_w_recv()
-    ab[plane] = jnp.sum(zb[...].astype(F32), axis=0).astype(BF)
-    ag_w_start()
     for q in (1, 2, 3):
         far_copy(q).wait_recv()
     lflat[...] = sa[zq] + rl[0].astype(F32) + rl[1].astype(F32) + rl[2].astype(F32)
     for i in range(32):
         lf[pl.ds(i, 8, stride=32), :] = lflat[:, 32 * i : 32 * i + 32]
     lo[...] = jnp.swapaxes(lf[...].reshape(8, 32, 32), 1, 2)
-    ag_w_recv()
+    for k in ACROSS[::-1]:
+        back_copy(k).wait_recv()
+        pass_on(k).start()
+    for k in range(CHIPS):
+        pass_on(k).wait_recv()
     wo[...] = ab[...].astype(F32).reshape(1024, 128) * (1.0 / 512)
 
-    for done in (ag_r_sent, rs_r_sent, rs_w_sent, z_w_sent, ag_w_sent):
+    for done in (ag_r_sent, rs_r_sent, z_w_sent):
         done()
+    halves.wait_send()
+    for k in ACROSS:
+        share_copy(k).wait_send()
+        back_copy(k).wait_send()
+    for k in range(CHIPS):
+        pass_on(k).wait_send()
     rest(lambda c: c.wait_send())
-    for d in (4, 8, 12):
+    for d in (FAR, ZS - FAR):
         left_arrived(d * XL, lambda c: c.wait_send())
-    for n in range(len(NEAR)):
+    for n in range(len(GROUP)):
         group_copy(n).wait_send()
     for q in (1, 2, 3):
         far_copy(q).wait_send()
@@ -367,8 +420,9 @@
             V((32, 8, 1024), BF), V((16, 16, 512), BF), V((256, 1024), BF), V((256, 512), BF), V((1024, 512), BF),
             V((4, 2, 4, 8, 1024), BF), V((7, 4, 8, 1024), BF), V((4, 8, 1024), F32), V((4, 8, 1024), BF), V((3, 8, 1024), BF),
             V((16, 16, 512), BF), V((16, 16, 512), BF),
-            V((32, 32, 128), BF), V((32, 32, 128), BF), V((16, 32, 128), BF), V((32, 32, 128), BF),
-            dma((4,)), dma((2, 32)), dma((2, 16)), dma((2, 7)), dma((2, 4)), dma((2, 16)), dma((2, 32)), dma((2, 16)), dma((2, 32)),
+            V((16, 32, 128), F32), V((16, 32, 128), F32), V((16, 32, 128), BF), V((16, 32, 128), BF), V((16, 32, 128), BF), V((2, 16, 32, 128), BF),
+            dma((4,)), dma((2, 32)), dma((2, 16)), dma((2, 7)), dma((2, 4)), dma((2, 16)),
+            dma((2,)), dma((2, 16)), dma((2, 16)), dma((2, 16)), dma((2, 16)),
         ],
         compiler_params=pltpu.CompilerParams(
             collective_id=0, has_side_effects=True, vmem_limit_bytes=24 << 20

time: 61.2 us -> 58.5 us (0.956)
  Pallas kernels: 60.4 us -> 57.7 us
    pallas_call x1, Pallas kernels: 59.5 us -> 56.8 us  [per_device(): pl.pallas_call(kernel, out_shape=[jax.ShapeDtypeStruct((8, 32, 32), F32),...]
where the time goes in v4:
time: 58.5 us; the launch traced here: 58.3 us
  Pallas kernels  57.7 us (99%)
  between operations  0.64 us (1%)
    pallas_call x1, Pallas kernels, per_device(): pl.pallas_call(kernel, out_shape=[jax.ShapeDtypeStruct((8, 32, 32), F32),...  56.8 us

profile of v4, /device:TPU:1, one launch (start us, length us, event | category | flops | bytes accessed | tf_op | source)
XLA Modules:
  0.0 58.3 jit_solution(6036673915091945359)
XLA Ops:
  0.6 56.8 %pair_backward.1 = (f32[8,32,32]{2,1,0:T(8,128)S(1)}, f32[16,16,32]{2,1,0:T(8,128)S(1)}, f32[1024,128]{1,0:T(8,128)S(1)}) custom-call(bf16[8,32,32]{2,1,0:T(8,128)(2,1)} %l_hbm.1, bf16[16,16,32]{2,1,0:T(8,128)(2,1)} %r_hbm.1, bf16[32,16,128]{2,1,0:T(8,128)(2,1)} %g_hbm.1, bf16[1024,128]{1,0:T(8,128)(2,1)} %w_hbm.1), custom_call_target="tpu_custom_call" | custom-call | flops 1073741824 | bytes 1048576 | tf_op jit(solution)/shard_map/pair_backward/pallas_call | solution.py:407
  57.4 0.9 %hand_over.1 = (f32[8,32,32]{2,1,0:T(8,128)}, f32[16,16,32]{2,1,0:T(8,128)}, f32[1024,128]{1,0:T(8,128)}) custom-call(f32[8,32,32]{2,1,0:T(8,128)S(1)} %get-tuple-element.6.l, f32[16,16,32]{2,1,0:T(8,128)S(1)} %get-tuple-element.7.r, f32[1024,128]{1,0:T(8,128)S(1)} %get-tuple-element.8.w), custom_call_target="tpu_custom_call" | custom-call | tf_op jit(solution)/shard_map/hand_over/pallas_call | solution.py:434

commit v5 on v4

--- a/solution.py
+++ b/solution.py
@@ -223,7 +223,7 @@
 
         return (
             lambda first=1, last=n: each(lambda c: c.start(), first, last),
-            lambda: each(lambda c: c.wait_recv(), 1, n),
+            lambda first=1, last=n: each(lambda c: c.wait_recv(), first, last),
             lambda: each(lambda c: c.wait_send(), 1, n),
         )
 
@@ -350,10 +350,11 @@
             device_id_type=MESH,
         )
 
+    z_w_recv(8, ZS)
     for q in (2, 1, 3):
         far_copy(q).start()
 
-    z_w_recv()
+    z_w_recv(1, 8)
     ab[core, chip] = jnp.sum(zb[...].astype(F32), axis=0).astype(BF)
     for k in ACROSS:
         back_copy(k).start()
@@ -362,15 +363,15 @@
     rflat[...] = jnp.sum(rr[...].astype(F32), axis=0)
     for j in range(16):
         ro[:, j, :] = rflat[:, 32 * j : 32 * j + 32]
+    for k in ACROSS[::-1]:
+        back_copy(k).wait_recv()
+        pass_on(k).start()
     for q in (1, 2, 3):
         far_copy(q).wait_recv()
     lflat[...] = sa[zq] + rl[0].astype(F32) + rl[1].astype(F32) + rl[2].astype(F32)
     for i in range(32):
         lf[pl.ds(i, 8, stride=32), :] = lflat[:, 32 * i : 32 * i + 32]
     lo[...] = jnp.swapaxes(lf[...].reshape(8, 32, 32), 1, 2)
-    for k in ACROSS[::-1]:
-        back_copy(k).wait_recv()
-        pass_on(k).start()
     for k in range(CHIPS):
         pass_on(k).wait_recv()
     wo[...] = ab[...].astype(F32).reshape(1024, 128) * (1.0 / 512)

time: 58.5 us -> 56.4 us (0.964)
  Pallas kernels: 57.7 us -> 55.6 us
    pallas_call x1, Pallas kernels: 56.8 us -> 54.7 us  [per_device(): pl.pallas_call(kernel, out_shape=[jax.ShapeDtypeStruct((8, 32, 32), F32),...]
where the time goes in v5:
time: 56.4 us; the launch traced here: 56.3 us
  Pallas kernels  55.6 us (99%)
  between operations  0.64 us (1%)
    pallas_call x1, Pallas kernels, per_device(): pl.pallas_call(kernel, out_shape=[jax.ShapeDtypeStruct((8, 32, 32), F32),...  54.7 us

profile of v5, /device:TPU:1, one launch (start us, length us, event | category | flops | bytes accessed | tf_op | source)
XLA Modules:
  0.0 56.3 jit_solution(9580432614478573476)
XLA Ops:
  0.6 54.7 %pair_backward.1 = (f32[8,32,32]{2,1,0:T(8,128)S(1)}, f32[16,16,32]{2,1,0:T(8,128)S(1)}, f32[1024,128]{1,0:T(8,128)S(1)}) custom-call(bf16[8,32,32]{2,1,0:T(8,128)(2,1)} %l_hbm.1, bf16[16,16,32]{2,1,0:T(8,128)(2,1)} %r_hbm.1, bf16[32,16,128]{2,1,0:T(8,128)(2,1)} %g_hbm.1, bf16[1024,128]{1,0:T(8,128)(2,1)} %w_hbm.1), custom_call_target="tpu_custom_call" | custom-call | flops 1073741824 | bytes 1048576 | tf_op jit(solution)/shard_map/pair_backward/pallas_call | solution.py:408
  55.4 0.9 %hand_over.1 = (f32[8,32,32]{2,1,0:T(8,128)}, f32[16,16,32]{2,1,0:T(8,128)}, f32[1024,128]{1,0:T(8,128)}) custom-call(f32[8,32,32]{2,1,0:T(8,128)S(1)} %get-tuple-element.6.l, f32[16,16,32]{2,1,0:T(8,128)S(1)} %get-tuple-element.7.r, f32[1024,128]{1,0:T(8,128)S(1)} %get-tuple-element.8.w), custom_call_target="tpu_custom_call" | custom-call | tf_op jit(solution)/shard_map/hand_over/pallas_call | solution.py:435

commit v6 on v5

--- a/solution.py
+++ b/solution.py
@@ -366,6 +366,12 @@
     for k in ACROSS[::-1]:
         back_copy(k).wait_recv()
         pass_on(k).start()
+
+    def write_half(h):
+        rows = pl.ds(pl.multiple_of(h * 512, 512), 512)
+        wo[rows, :] = ab[h].astype(F32).reshape(512, 128) * (1.0 / 512)
+
+    write_half(core)
     for q in (1, 2, 3):
         far_copy(q).wait_recv()
     lflat[...] = sa[zq] + rl[0].astype(F32) + rl[1].astype(F32) + rl[2].astype(F32)
@@ -374,7 +380,7 @@
     lo[...] = jnp.swapaxes(lf[...].reshape(8, 32, 32), 1, 2)
     for k in range(CHIPS):
         pass_on(k).wait_recv()
-    wo[...] = ab[...].astype(F32).reshape(1024, 128) * (1.0 / 512)
+    write_half(1 - core)
 
     for done in (ag_r_sent, rs_r_sent, z_w_sent):
         done()

time: 56.4 us -> 56.4 us (level)
  no operation moved by 1% of the time
where the time goes in v6:
time: 56.4 us; the launch traced here: 56.3 us
  Pallas kernels  55.6 us (99%)
  between operations  0.64 us (1%)
    pallas_call x1, Pallas kernels, per_device(): pl.pallas_call(kernel, out_shape=[jax.ShapeDtypeStruct((8, 32, 32), F32),...  54.7 us

profile of v6, /device:TPU:1, one launch (start us, length us, event | category | flops | bytes accessed | tf_op | source)
XLA Modules:
  0.0 56.3 jit_solution(3348472089570418812)
XLA Ops:
  0.6 54.7 %pair_backward.1 = (f32[8,32,32]{2,1,0:T(8,128)S(1)}, f32[16,16,32]{2,1,0:T(8,128)S(1)}, f32[1024,128]{1,0:T(8,128)S(1)}) custom-call(bf16[8,32,32]{2,1,0:T(8,128)(2,1)} %l_hbm.1, bf16[16,16,32]{2,1,0:T(8,128)(2,1)} %r_hbm.1, bf16[32,16,128]{2,1,0:T(8,128)(2,1)} %g_hbm.1, bf16[1024,128]{1,0:T(8,128)(2,1)} %w_hbm.1), custom_call_target="tpu_custom_call" | custom-call | flops 1073741824 | bytes 1048576 | tf_op jit(solution)/shard_map/pair_backward/pallas_call | solution.py:414
  55.4 0.9 %hand_over.1 = (f32[8,32,32]{2,1,0:T(8,128)}, f32[16,16,32]{2,1,0:T(8,128)}, f32[1024,128]{1,0:T(8,128)}) custom-call(f32[8,32,32]{2,1,0:T(8,128)S(1)} %get-tuple-element.6.l, f32[16,16,32]{2,1,0:T(8,128)S(1)} %get-tuple-element.7.r, f32[1024,128]{1,0:T(8,128)S(1)} %get-tuple-element.8.w), custom_call_target="tpu_custom_call" | custom-call | tf_op jit(solution)/shard_map/hand_over/pallas_call | solution.py:441
